TPU v7x, 256 devices: a whole 4x4x8 slice. The times are simulated.
256 devices in a mesh: row: 32 (over x, y, core), col: 8 (over z).
Axes of the slice: x: 4, y: 4, z: 8, core: 2. Of those that a mesh axis runs over, the one named last changes fastest.
Arguments:
- source: bfloat16 [32768, 128], P(('row', 'col')), may hold values from -10 to 10
- target: bfloat16 [32768, 128], P(('col', 'row')), may hold values from -80 to 80
- target_potential: bfloat16 [32768], P(('col', 'row')), may hold values from -4 to 4
- prev_moment: float32 [128, 128], replicated, may hold values from -0.1 to 0.5
Outputs:
- moment: float32 [128, 128], replicated
- source_potential: float32 [32768], P('row')
- target_update: float32 [32768], P(('col', 'row'))
All inputs are finite; a program needn't handle non-finite values.
Results may differ from a plain program's by a relative error of at most 0.0059.
Values may be sent and summed in bfloat16 or wider, within the bound.
A program may use at most 64 MiB of HBM per device.

v0:
```python
import math

import jax
import jax.numpy as jnp
from jax import lax
from jax.sharding import PartitionSpec as P

ITERS = 2


def project(rows_block, matrix):
    return jnp.dot(rows_block.astype(jnp.float32), matrix, precision=lax.Precision.HIGHEST).astype(
        jnp.bfloat16
    )


def tile_costs(projected, cols_block):
    return -4.0 * lax.dot_general(
        projected, cols_block, (((1,), (1,)), ((), ())), preferred_element_type=jnp.float32
    )


def row_totals(scores):
    top_score = lax.pmax(jnp.max(scores, axis=1), "col")
    mass_total = lax.psum(jnp.sum(jnp.exp(scores - top_score[:, None]), axis=1), "col")
    return top_score + jnp.log(mass_total)


def column_totals(scores):
    top_score = lax.pmax(jnp.max(scores, axis=0), "row")
    mass_total = lax.psum(jnp.sum(jnp.exp(scores - top_score[None, :]), axis=0), "row")
    return top_score + jnp.log(mass_total)


def per_device(source, target, target_potential, prev_moment):
    rows_block = lax.all_gather(source, "col", axis=0, tiled=True)
    cols_block, potential = (
        lax.all_gather(target, "row", axis=0, tiled=True),
        lax.all_gather(target_potential, "row", axis=0, tiled=True),
    )
    row_devices = lax.axis_size("row")
    rows_total = rows_block.shape[0] * row_devices
    cols_total = cols_block.shape[0] * lax.axis_size("col")
    share_width = cols_block.shape[0] // row_devices
    position = lax.axis_index("row")
    column = potential.astype(jnp.float32)
    scores = column[None, :] - tile_costs(project(rows_block, prev_moment), cols_block)
    spread = row_totals(scores)
    weights = (jnp.exp(scores - spread[:, None]) / rows_total).astype(jnp.bfloat16)
    carried = jnp.dot(weights, cols_block, preferred_element_type=jnp.float32)
    partial_moment = lax.dot_general(
        rows_block.astype(jnp.float32),
        carried,
        (((0,), (0,)), ((), ())),
        precision=lax.Precision.HIGHEST,
    )
    moment = lax.psum(partial_moment, ("row", "col"))
    cost_tile = tile_costs(project(rows_block, moment), cols_block)
    source_potential = jnp.zeros((rows_block.shape[0],), jnp.float32)
    own_share = jnp.zeros((share_width,), jnp.float32)
    for iteration in range(ITERS):
        source_potential = math.log(cols_total) - row_totals(column[None, :] - cost_tile)
        column_scores = source_potential[:, None] - cost_tile
        column = math.log(rows_total) - column_totals(column_scores)
        own_share = lax.dynamic_slice_in_dim(column, position * share_width, share_width)
    return (moment, source_potential, own_share)


def solution(mesh):
    placed = (P(("row", "col"), None), P(("col", "row"), None), P(("col", "row")), P())
    return jax.shard_map(
        per_device,
        mesh=mesh,
        in_specs=placed,
        out_specs=(P(), P("row"), P(("col", "row"))),
        check_vma=False,
    )
```

profile of v0, /device:TPU:1, one launch (start us, length us, event | category | flops | bytes accessed | tf_op | source)
XLA Modules:
  0.0 976.0 jit_solution(412638877074749381)
XLA Ops:
  7.2 0.7 all-gather.3.cloned.1.call-update
  7.9 0.0 all-reduce.2.cloned.1.call-start
  8.0 23.1 %all-gather = bf16[32,1,128]{2,1,0:T(2,128)(2,1)S(1)} all-gather(bf16[1,1,128]{2,1,0:T(2,128)(2,1)} %bitcast.20), channel_id=1, replica_groups=mesh['row'=32,'col'=8] {'row'}, dimensions={0}, use_global_device_ids=true | all-gather | bytes 8448 | tf_op jit(solution)/shard_map/all_gather | solution.py:39
  31.1 22.5 %all_gather.10 = bf16[1024,128]{1,0:T(8,128)(2,1)S(1)} all-gather(bf16[128,128]{1,0:T(8,128)(2,1)} %param.4), channel_id=1, replica_groups=mesh['row'=32,'col'=8] {'col'}, dimensions={0}, use_global_device_ids=true | all-gather | bytes 294912 | tf_op jit(solution)/shard_map/all_gather | solution.py:36
  53.6 0.4 convolution_convert_fusion.1
  53.9 8.7 all-gather.3.cloned.1.call-done
  62.6 8.3 fusion
  71.0 13.8 %pmax.35 = f32[1024]{0:T(1024)S(1)} all-reduce(f32[1024]{0:T(1024)S(1)} %get-tuple-element.9), channel_id=1, replica_groups=mesh['row'=32,'col'=8] {'col'}, use_global_device_ids=true, to_apply=%region_1.0 | all-reduce | flops 1024 | bytes 8192 | tf_op jit(solution)/shard_map/pmax | solution.py:24
  84.8 7.8 exponential_reduce_fusion.4
  92.6 11.2 %psum.42 = f32[1024]{0:T(1024)S(1)} all-reduce(f32[1024]{0:T(1024)S(1)} %exponential_reduce_fusion.4), channel_id=1, replica_groups=mesh['row'=32,'col'=8] {'col'}, use_global_device_ids=true, to_apply=%region_3.0 | all-reduce | flops 1024 | bytes 8192 | tf_op jit(solution)/shard_map/psum | solution.py:25
  103.8 7.8 fusion.1
  111.6 1.2 convolution_bitcast_fusion
  112.9 242.5 %all-reduce.2.cloned.1.call-done = f32[128,128]{0,1:T(8,128)} async-done(((f32[128,128]{0,1:T(8,128)}), f32[128,128]{0,1:T(8,128)}) %all-reduce.2.cloned.1.call-update) | async-done | bytes 65552 | tf_op jit(solution)/shard_map/psum | solution.py:57
  355.4 1.2 convolution_convert_fusion
  356.6 7.0 subtract_reduce_fusion.3
  363.6 12.8 %pmax.36 = f32[1024]{0:T(1024)S(1)} all-reduce(f32[1024]{0:T(1024)S(1)} %get-tuple-element.11), channel_id=1, replica_groups=mesh['row'=32,'col'=8] {'col'}, use_global_device_ids=true, to_apply=%region_6.0 | all-reduce | flops 1024 | bytes 8192 | tf_op jit(solution)/shard_map/pmax | solution.py:24
  376.4 7.8 exponential_reduce_fusion.3
  384.2 10.7 %psum.44 = f32[1024]{0:T(1024)S(1)} all-reduce(f32[1024]{0:T(1024)S(1)} %exponential_reduce_fusion.3), channel_id=1, replica_groups=mesh['row'=32,'col'=8] {'col'}, use_global_device_ids=true, to_apply=%region_8.0 | all-reduce | flops 1024 | bytes 8192 | tf_op jit(solution)/shard_map/psum | solution.py:25
  394.9 7.7 subtract_reduce_fusion.2
  402.6 125.0 %pmax.37 = f32[4096]{0:T(1024)S(1)} all-reduce(f32[4096]{0:T(1024)S(1)} %subtract_reduce_fusion.2), channel_id=1, replica_groups=mesh['row'=32,'col'=8] {'row'}, use_global_device_ids=true, to_apply=%region_10.0 | all-reduce | flops 4096 | bytes 32768 | tf_op jit(solution)/shard_map/pmax | solution.py:30
  527.6 7.7 exponential_reduce_fusion.2
  535.3 123.8 %psum.45 = f32[4096]{0:T(1024)S(1)} all-reduce(f32[4096]{0:T(1024)S(1)} %exponential_reduce_fusion.2), channel_id=1, replica_groups=mesh['row'=32,'col'=8] {'row'}, use_global_device_ids=true, to_apply=%region_12.0 | all-reduce | flops 4096 | bytes 32768 | tf_op jit(solution)/shard_map/psum | solution.py:31
  659.1 7.5 subtract_reduce_fusion.1
  666.6 11.4 %pmax.38 = f32[1024]{0:T(1024)S(1)} all-reduce(f32[1024]{0:T(1024)S(1)} %subtract_reduce_fusion.1), channel_id=1, replica_groups=mesh['row'=32,'col'=8] {'col'}, use_global_device_ids=true, to_apply=%region_14.0 | all-reduce | flops 1024 | bytes 8192 | tf_op jit(solution)/shard_map/pmax | solution.py:24
  678.0 7.8 exponential_reduce_fusion.1
  685.9 11.4 %psum.46 = f32[1024]{0:T(1024)S(1)} all-reduce(f32[1024]{0:T(1024)S(1)} %exponential_reduce_fusion.1), channel_id=1, replica_groups=mesh['row'=32,'col'=8] {'col'}, use_global_device_ids=true, to_apply=%region_16.0 | all-reduce | flops 1024 | bytes 8192 | tf_op jit(solution)/shard_map/psum | solution.py:25
  697.3 7.8 subtract_reduce_fusion
  705.0 131.3 %pmax.39 = f32[4096]{0:T(1024)S(1)} all-reduce(f32[4096]{0:T(1024)S(1)} %subtract_reduce_fusion), channel_id=1, replica_groups=mesh['row'=32,'col'=8] {'row'}, use_global_device_ids=true, to_apply=%region_18.0 | all-reduce | flops 4096 | bytes 32768 | tf_op jit(solution)/shard_map/pmax | solution.py:30
  836.3 7.7 exponential_reduce_fusion
  844.1 123.8 %psum.47 = f32[4096]{0:T(1024)S(1)} all-reduce(f32[4096]{0:T(1024)S(1)} %exponential_reduce_fusion), channel_id=1, replica_groups=mesh['row'=32,'col'=8] {'row'}, use_global_device_ids=true, to_apply=%region_20.0 | all-reduce | flops 4096 | bytes 32768 | tf_op jit(solution)/shard_map/psum | solution.py:31
  967.9 0.6 fusion.2
  968.5 0.7 copy.8
  (15 shorter events, 0.1 us)
Async XLA Ops:
  7.2 46.4 %copy-start = (f32[128,128]{1,0:T(8,128)S(1)}, f32[128,128]{1,0:T(8,128)}, u32[]{:S(2)}) copy-start(f32[128,128]{1,0:T(8,128)} %param.7) | copy-start | bytes 196612
  7.2 55.4 %all-gather.3.cloned.1.call-start = ((), (), s32[]{:S(2)}) async-start(), calls=%async_computation | async-start | bytes 1081344 | tf_op jit(solution)/shard_map/all_gather | solution.py:38
  7.9 347.4 %all-reduce.2.cloned.1.call-start = ((), (), s32[]{:S(2)}) async-start(), calls=%async_computation.1 | async-start | bytes 131072 | tf_op jit(solution)/shard_map/psum | solution.py:57
  62.6 41.2 %copy-start.1 = (bf16[4096,128]{1,0:T(8,128)(2,1)S(1)}, bf16[4096,128]{1,0:T(8,128)(2,1)}, u32[]{:S(2)}) copy-start(bf16[4096,128]{1,0:T(8,128)(2,1)} %all-gather.3.cloned.1.call-done) | copy-start | bytes 3145732
  697.3 146.8 %copy-start.3 = (f32[1024]{0:T(1024)}, f32[1024]{0:T(1024)S(1)}, u32[]{:S(2)}) copy-start(f32[1024]{0:T(1024)S(1)} %add_subtract_fusion.1) | copy-start | bytes 12292
  697.3 271.2 %copy-start.2 = (f32[128,128]{0,1:T(8,128)S(1)}, f32[128,128]{0,1:T(8,128)}, u32[]{:S(2)}) copy-start(f32[128,128]{0,1:T(8,128)} %all-reduce.2.cloned.1.call-done) | copy-start | bytes 196612
Sparse Core Ops, SparseCore 0:
  10.6 52.0 all-gather.2
  113.0 242.3 all-reduce.1
where the time goes:
time: 980 us; the launch traced here: 976 us
  blocking collectives  621 us (63%)
  waiting for transfers between devices  252 us (26%)
  other arithmetic  62.6 us (6%)
  matrix products  25.9 us (3%)
  between operations  14.1 us (1%)
    pmax x2, blocking collectives, column_totals(): top_score = lax.pmax(jnp.max(scores, axis=0), 'row')  256 us
    psum x2, blocking collectives, column_totals(): lax.psum(jnp.sum(jnp.exp(scores - top_score[None, :]), axis=0), 'row')  248 us
    psum x1, waiting for transfers between devices, per_device(): moment = lax.psum(partial_moment, ('row', 'col'))  242 us
    pmax x3, blocking collectives, row_totals(): top_score = lax.pmax(jnp.max(scores, axis=1), 'col')  38 us
    psum x3, blocking collectives, row_totals(): lax.psum(jnp.sum(jnp.exp(scores - top_score[:, None]), axis=1), 'col')  33.3 us
    reduce_sum x3, other arithmetic, row_totals(): jnp.sum(jnp.exp(scores - top_score[:, None]), axis=1)  23.5 us
    all_gather x1, blocking collectives, per_device(): lax.all_gather(target_potential, 'row', axis=0, tiled=True)  23.1 us
    all_gather x1, blocking collectives, per_device(): rows_block = lax.all_gather(source, 'col', axis=0, tiled=True)  22.5 us
  transfers between devices with their start and end apart: 2, of which 2 were waited for; matrix products, arithmetic and copies ran while one was open for 0% of the time, Pallas kernels for 0%

commit v1 on v0

v1 whole, which is shorter than its diff:
```python
import math

import jax
import jax.numpy as jnp
from jax import lax
from jax.experimental import pallas as pl
from jax.experimental.pallas import tpu as pltpu
from jax.sharding import PartitionSpec as P

MESH = pl.DeviceIdType.MESH
F32, BF16 = jnp.float32, jnp.bfloat16
D = 128
ROWS = 32
COLS = 8
NR = 1024
NC = 4096
N = 32768
LOG_N = math.log(N)
PAD = 144
TC = 512
RC = 256
CC = 512

NT_DIMS = (((1,), (1,)), ((), ()))
TN_DIMS = (((0,), (0,)), ((), ()))


def split3(value):
    high = value.astype(BF16)
    rest = value - high.astype(F32)
    middle = rest.astype(BF16)
    return high, middle, (rest - middle.astype(F32)).astype(BF16)


def dot_nt(a, b):
    return lax.dot_general(a, b, NT_DIMS, preferred_element_type=F32)


def dot_nn(a, b):
    return jnp.dot(a, b, preferred_element_type=F32)


def kernel(
    source_ref, target_ref, potential_ref, prev_ref,
    moment_ref, row_out_ref, col_out_ref,
    src, tbuf, taug, paug, tile, kernel_tile, frep, chunk_top, col_top, col_mass,
    stage_row, row_in1, row_in2, row_in3,
    mom_stage, mom_in, own_mom, mom_z, mom_all,
    stage_col, col_in, col_in2, col_all, own_col,
    src_send, src_recv, t_send, t_recv, f_send,
    send_sem, recv_sem,
):
    me_r = lax.axis_index("row")
    me_z = lax.axis_index("col")
    core = lax.rem(me_r, 2)
    chip = lax.div(me_r, 2)
    sibling = chip * 2 + (1 - core)

    def row_peer(k):
        return lax.rem(me_r + k, ROWS)

    def z_peer(k):
        return lax.rem(me_z + k, COLS)

    def plane_peer(k):
        return lax.rem(chip + k, ROWS // 2) * 2 + core

    def remote(source, dest, send, recv, row, col):
        return pltpu.make_async_remote_copy(
            src_ref=source, dst_ref=dest, send_sem=send, recv_sem=recv,
            device_id=(row, col), device_id_type=MESH,
        )

    def settle(buffer, sem):
        pltpu.make_async_copy(buffer, buffer, sem).wait()

    barrier = pltpu.get_barrier_semaphore()

    def greet_row(k, _):
        pl.semaphore_signal(barrier, inc=1, device_id=(row_peer(k), me_z), device_id_type=MESH)
        return _

    def greet_z(k, _):
        pl.semaphore_signal(barrier, inc=1, device_id=(me_r, z_peer(k)), device_id_type=MESH)
        return _

    lax.fori_loop(1, ROWS, greet_row, 0)
    lax.fori_loop(1, COLS, greet_z, 0)
    src[me_z] = source_ref[...]
    tbuf[me_r, 0:D] = target_ref[...]
    tbuf[me_r, D:PAD] = jnp.broadcast_to(potential_ref[...], (PAD - D, D)).astype(BF16)
    paug[:, D:] = jnp.ones((NR, D), BF16)
    pl.semaphore_wait(barrier, ROWS + COLS - 2)

    def send_source(k, _):
        remote(src.at[me_z], src.at[me_z], src_send, src_recv, me_r, z_peer(k)).start()
        return _

    def send_target(k, _):
        remote(tbuf.at[me_r], tbuf.at[me_r], t_send, t_recv.at[me_r], plane_peer(k), me_z).start()
        return _

    remote(tbuf.at[me_r], tbuf.at[me_r], f_send, t_recv.at[me_r], sibling, me_z).start()
    lax.fori_loop(1, COLS, send_source, 0)
    lax.fori_loop(1, ROWS // 2, send_target, 0)

    def forward(k, _):
        slot = plane_peer(k)
        settle(tbuf.at[slot], t_recv.at[slot])
        remote(tbuf.at[slot], tbuf.at[slot], f_send, t_recv.at[slot], sibling, me_z).start()
        return _

    lax.fori_loop(1, ROWS // 2, forward, 0)

    settle(src.at[pl.ds(0, COLS - 1)], src_recv)
    settle(src.at[pl.ds(0, COLS - 1)], src_send)

    def project(parts):
        rows = src[...].reshape(NR, D)
        total = parts(rows)
        paug[:, 0:D] = (4.0 * total).astype(BF16)

    def project_prev(rows):
        high, middle, low = split3(prev_ref[...])
        return dot_nn(rows, high) + (dot_nn(rows, middle) + dot_nn(rows, low))

    project(project_prev)

    def arrive(k, _):
        slot = lax.rem(chip + k, ROWS // 2) * 2 + (1 - core)
        settle(tbuf.at[slot], t_recv.at[slot])
        return _

    lax.fori_loop(0, ROWS // 2, arrive, 0)
    settle(tbuf.at[pl.ds(0, ROWS // 2 - 1)], t_send)
    settle(tbuf.at[pl.ds(0, ROWS // 2)], f_send)

    eye = lax.broadcasted_iota(jnp.int32, (D, D), 0) == lax.broadcasted_iota(jnp.int32, (D, D), 1)

    def place(k, _):
        block = tbuf[k]
        at = pl.ds(pl.multiple_of(k * D, D), D)
        taug[at, 0:D] = block[0:D]
        taug[at, D:] = jnp.where(eye, block[D : D + 1].astype(F32), 0.0).astype(BF16)
        return _

    lax.fori_loop(0, ROWS, place, 0)

    def row_pass(keep):
        def step(c, carry):
            top, mass = carry
            at = pl.ds(pl.multiple_of(c * TC, TC), TC)
            scores = dot_nt(taug[at, :], paug[...])
            here = jnp.max(scores, axis=0, keepdims=True)
            weights = jnp.exp(scores - here)
            if keep:
                tile[at, :] = weights.astype(BF16)
                chunk_top[c] = here
            new_top = jnp.maximum(top, here)
            mass = mass * jnp.exp(top - new_top) + jnp.sum(weights, axis=0, keepdims=True) * jnp.exp(here - new_top)
            return new_top, mass

        start = (jnp.full((1, NR), -jnp.inf, F32), jnp.zeros((1, NR), F32))
        return lax.fori_loop(0, NC // TC, step, start)

    def send_z(stage, inbox, channel):
        def one(k, _):
            remote(stage, inbox.at[me_z], send_sem.at[channel], recv_sem.at[channel], me_r, z_peer(k)).start()
            return _

        lax.fori_loop(1, COLS, one, 0)
        inbox[me_z] = stage[...]

    def wait_z(inbox, channel):
        settle(inbox.at[pl.ds(0, COLS - 1)], recv_sem.at[channel])
        settle(inbox.at[pl.ds(0, COLS - 1)], send_sem.at[channel])

    def total_lse(inbox):
        values = inbox[...]
        top = jnp.max(values, axis=0)
        return top + jnp.log(jnp.sum(jnp.exp(values - top[None]), axis=0))

    top, mass = row_pass(True)
    stage_row[...] = top + jnp.log(mass)
    send_z(stage_row, row_in1, 0)

    def carry_step(c, total):
        at = pl.ds(pl.multiple_of(c * TC, TC), TC)
        part = lax.dot_general(taug[at, 0:D], tile[at, :], TN_DIMS, preferred_element_type=F32)
        return total + part * jnp.exp(chunk_top[c] - top)

    carried = lax.fori_loop(0, NC // TC, carry_step, jnp.zeros((D, NR), F32))
    wait_z(row_in1, 0)
    carried = carried * (jnp.exp(top - total_lse(row_in1)) / N)
    rows = src[...].reshape(NR, D)
    high, middle, low = split3(carried)
    part_moment = dot_nn(high, rows) + (dot_nn(middle, rows) + dot_nn(low, rows))
    for k in range(ROWS):
        mom_stage[k] = part_moment[4 * k : 4 * k + 4]

    def send_moment(k, _):
        peer = row_peer(k)
        remote(mom_stage.at[peer], mom_in.at[me_r], send_sem.at[1], recv_sem.at[1], peer, me_z).start()
        return _

    lax.fori_loop(1, ROWS, send_moment, 0)
    mom_in[me_r] = mom_stage[me_r]
    settle(mom_in.at[pl.ds(0, ROWS - 1)], recv_sem.at[1])
    settle(mom_in.at[pl.ds(0, ROWS - 1)], send_sem.at[1])
    own_mom[0] = jnp.sum(mom_in[...], axis=0)
    send_z(own_mom.at[0], mom_z, 2)
    wait_z(mom_z, 2)
    own_mom[1] = jnp.sum(mom_z[...], axis=0)

    def share_moment(k, _):
        remote(own_mom.at[1], mom_all.at[me_r], send_sem.at[3], recv_sem.at[3], row_peer(k), me_z).start()
        return _

    lax.fori_loop(1, ROWS, share_moment, 0)
    mom_all[me_r] = own_mom[1]
    settle(mom_all.at[pl.ds(0, ROWS - 1)], recv_sem.at[3])
    settle(mom_all.at[pl.ds(0, ROWS - 1)], send_sem.at[3])
    for k in range(ROWS):
        moment_ref[4 * k : 4 * k + 4, :] = mom_all[k]
    moment_t = moment_ref[...]

    def project_new(block):
        first, second, third = split3(moment_t)
        return dot_nt(block, first) + (dot_nt(block, second) + dot_nt(block, third))

    project(project_new)
    moment_ref[...] = moment_t.T

    top, mass = row_pass(False)
    stage_row[...] = top + jnp.log(mass)
    send_z(stage_row, row_in2, 4)
    wait_z(row_in2, 4)
    first_row = LOG_N - total_lse(row_in2)

    for k in range(NR // D):
        frep[k * D : (k + 1) * D, :] = jnp.broadcast_to(first_row[:, k * D : (k + 1) * D], (D, D)).T

    def col_step(step, _):
        r = lax.div(step, NC // CC)
        c = lax.rem(step, NC // CC)
        rows_at = pl.ds(pl.multiple_of(r * RC, RC), RC)
        cols_at = pl.ds(pl.multiple_of(c * CC, CC), CC)
        shift = frep[rows_at, :]
        scores = dot_nt(paug[rows_at, 0:D], taug[cols_at, 0:D]) + jnp.concatenate([shift] * (CC // D), axis=1)
        here = jnp.max(scores, axis=0, keepdims=True)
        weights = jnp.exp(scores - here)
        kernel_tile[rows_at, cols_at] = weights.astype(BF16)
        col_top[r, :, cols_at] = here
        col_mass[r, :, cols_at] = jnp.sum(weights, axis=0, keepdims=True)
        return _

    lax.fori_loop(0, (NR // RC) * (NC // CC), col_step, 0)
    tops = col_top[...]
    best = jnp.max(tops, axis=0)
    stage_col[0] = best + jnp.log(jnp.sum(col_mass[...] * jnp.exp(tops - best[None]), axis=0))

    def lanes(k):
        return pl.ds(pl.multiple_of(k * D, D), D)

    def scatter_cols(index, inbox, channel):
        def one(k, _):
            peer = row_peer(k)
            remote(
                stage_col.at[index, :, lanes(peer)], inbox.at[me_r],
                send_sem.at[channel], recv_sem.at[channel], peer, me_z,
            ).start()
            return _

        lax.fori_loop(1, ROWS, one, 0)
        inbox[me_r] = stage_col[index, :, lanes(me_r)]
        settle(inbox.at[pl.ds(0, ROWS - 1)], recv_sem.at[channel])
        settle(inbox.at[pl.ds(0, ROWS - 1)], send_sem.at[channel])

    scatter_cols(0, col_in, 5)
    own_col[...] = LOG_N - total_lse(col_in)

    def share_col(k, _):
        remote(own_col, col_all.at[:, lanes(me_r)], send_sem.at[6], recv_sem.at[6], row_peer(k), me_z).start()
        return _

    lax.fori_loop(1, ROWS, share_col, 0)
    col_all[:, lanes(me_r)] = own_col[...]
    settle(col_all.at[:, pl.ds(0, NC - D)], recv_sem.at[6])
    settle(col_all.at[:, pl.ds(0, NC - D)], send_sem.at[6])

    first_col = col_all[...]
    line = lax.broadcasted_iota(jnp.int32, (16, 1), 0)
    lhs = jnp.zeros((16, NC), F32)
    for r in range(NR // RC):
        factor = jnp.exp(first_col + col_top[r])
        col_mass[r] = factor
        for p, piece in enumerate(split3(factor)):
            lhs = jnp.where(line == 3 * r + p, piece.astype(F32), lhs)
    sums = dot_nt(lhs.astype(BF16), kernel_tile[...])
    for r in range(NR // RC):
        at = slice(r * RC, (r + 1) * RC)
        stage_row[:, at] = (
            sums[3 * r : 3 * r + 1, at] + (sums[3 * r + 1 : 3 * r + 2, at] + sums[3 * r + 2 : 3 * r + 3, at])
        )
    send_z(stage_row, row_in3, 7)
    wait_z(row_in3, 7)
    row_sum = jnp.sum(row_in3[...], axis=0)
    row_out_ref[...] = first_row + (LOG_N - jnp.log(row_sum))
    high, middle, low = split3(N / row_sum)
    scale = jnp.where(
        line == 0, high.astype(F32), jnp.where(line == 1, middle.astype(F32), jnp.where(line == 2, low.astype(F32), 0.0))
    ).astype(BF16)
    total = jnp.zeros((1, NC), F32)
    for r in range(NR // RC):
        at = slice(r * RC, (r + 1) * RC)
        part = dot_nn(scale[:, at], kernel_tile[at, :])
        total = total + (part[0:1] + (part[1:2] + part[2:3])) * col_mass[r]
    stage_col[1] = total
    scatter_cols(1, col_in2, 8)
    col_out_ref[...] = own_col[...] + (LOG_N - jnp.log(jnp.sum(col_in2[...], axis=0)))


def per_device(source, target, target_potential, prev_moment):
    vmem = pl.BlockSpec(memory_space=pltpu.VMEM)
    dma = pltpu.SemaphoreType.DMA
    moment, row, col = pl.pallas_call(
        kernel,
        out_shape=(
            jax.ShapeDtypeStruct((D, D), F32),
            jax.ShapeDtypeStruct((1, NR), F32),
            jax.ShapeDtypeStruct((1, D), F32),
        ),
        in_specs=[vmem] * 4,
        out_specs=(vmem,) * 3,
        scratch_shapes=[
            pltpu.VMEM((COLS, D, D), BF16),
            pltpu.VMEM((ROWS, PAD, D), BF16),
            pltpu.VMEM((NC, 2 * D), BF16),
            pltpu.VMEM((NR, 2 * D), BF16),
            pltpu.VMEM((NC, NR), BF16),
            pltpu.VMEM((NR, NC), BF16),
            pltpu.VMEM((NR, D), F32),
            pltpu.VMEM((NC // TC, 1, NR), F32),
            pltpu.VMEM((NR // RC, 1, NC), F32),
            pltpu.VMEM((NR // RC, 1, NC), F32),
            pltpu.VMEM((1, NR), F32),
            pltpu.VMEM((COLS, 1, NR), F32),
            pltpu.VMEM((COLS, 1, NR), F32),
            pltpu.VMEM((COLS, 1, NR), F32),
            pltpu.VMEM((ROWS, 4, D), F32),
            pltpu.VMEM((ROWS, 4, D), F32),
            pltpu.VMEM((2, 4, D), F32),
            pltpu.VMEM((COLS, 4, D), F32),
            pltpu.VMEM((ROWS, 4, D), F32),
            pltpu.VMEM((2, 1, NC), F32),
            pltpu.VMEM((ROWS, 1, D), F32),
            pltpu.VMEM((ROWS, 1, D), F32),
            pltpu.VMEM((1, NC), F32),
            pltpu.VMEM((1, D), F32),
            dma, dma, dma, dma((ROWS,)), dma,
            dma((9,)), dma((9,)),
        ],
        compiler_params=pltpu.CompilerParams(
            collective_id=0, has_side_effects=True, vmem_limit_bytes=58 << 20
        ),
    )(source, target, target_potential.astype(F32).reshape(1, D), prev_moment)
    return moment, row.reshape(NR), col.reshape(D)


def solution(mesh):
    placed = (P(("row", "col"), None), P(("col", "row"), None), P(("col", "row")), P())
    return jax.shard_map(
        per_device,
        mesh=mesh,
        in_specs=placed,
        out_specs=(P(), P("row"), P(("col", "row"))),
        check_vma=False,
    )
```

time: 980 us -> 101 us (0.10)
  blocking collectives: 621 us -> 0 us
  waiting for transfers between devices: 252 us -> 0 us
  Pallas kernels: 0 us -> 96.7 us
  other arithmetic: 62.6 us -> 1.17 us
  matrix products: 25.9 us -> 0 us
  between operations: 14.1 us -> 0.65 us
    pmax x5 -> x0, blocking collectives: 294 us -> none  [the longest x2 256 us: column_totals(): top_score = lax.pmax(jnp.max(scores, axis=0), 'row')]
    psum x5 -> x0, blocking collectives: 281 us -> none  [the longest x2 248 us: column_totals(): lax.psum(jnp.sum(jnp.exp(scores - top_score[None, :]), axis=0), 'row')]
    psum x1 -> x0, waiting for transfers between devices: 242 us -> none  [per_device(): moment = lax.psum(partial_moment, ('row', 'col'))]
    pallas_call x0 -> x1, Pallas kernels: none -> 96.7 us  [per_device(): pl.pallas_call(kernel, out_shape=(jax.ShapeDtypeStruct((D, D), F32), jax....]
    all_gather x2 -> x0, blocking collectives: 45.6 us -> none  [the longest x1 23.1 us: per_device(): lax.all_gather(target_potential, 'row', axis=0, tiled=True)]
    reduce_sum x5 -> x0, other arithmetic: 39 us -> none  [the longest x3 23.5 us: row_totals(): jnp.sum(jnp.exp(scores - top_score[:, None]), axis=1)]
    dot_general x6 -> x0, matrix products: 25.9 us -> none  [the longest x2 15.3 us: tile_costs(): lax.dot_general(projected, cols_block, (((1,), (1,)), ((), ())), preferre...]
    reduce_max x3 -> x0, other arithmetic: 23 us -> none  [the longest x2 15.5 us: column_totals(): top_score = lax.pmax(jnp.max(scores, axis=0), 'row')]
  transfers between devices with their start and end apart: 2 -> 0, of which waited for: 2 -> 0; matrix products, arithmetic and copies ran while one was open for 0% -> 0% of each run, Pallas kernels for 0% -> 0%
where the time goes in v1:
time: 101 us
  Pallas kernels  96.7 us (96%)
  local copies, waits for them, and re-layouts  2.59 us (3%)
  other arithmetic  1.17 us (1%)
    pallas_call x1, Pallas kernels, per_device(): pl.pallas_call(kernel, out_shape=(jax.ShapeDtypeStruct((D, D), F32), jax....  96.7 us
    unnamed x7, local copies, waits for them, and re-layouts  2.59 us

profile of v1, /device:TPU:1, one launch (start us, length us, event | category | flops | bytes accessed | tf_op | source)
XLA Modules:
  0.0 101.1 jit_solution(5351417462572241122)
XLA Ops:
  0.6 1.2 %bitcast_convert_fusion.potential_ref = f32[1,128]{1,0:T(1,128)} fusion(bf16[128]{0:T(256)(128)(2,1)} %param.6), kind=kLoop, calls=%fused_computation | loop fusion | flops 128 | bytes 768 | tf_op jit(solution)/shard_map/reshape | solution.py:366
  1.8 96.7 %shard_map.67 = (f32[128,128]{1,0:T(8,128)}, f32[1,1024]{1,0:T(1,128)}, f32[1,128]{1,0:T(1,128)}) custom-call(bf16[128,128]{1,0:T(8,128)(2,1)} %source_ref.1, bf16[128,128]{1,0:T(8,128)(2,1)} %target_ref.1, f32[1,128]{1,0:T(1,128)} %bitcast_convert_fusion.potential_ref, f32[128,128]{1,0:T(8,128)} %prev_ref.1), custom_call_target="tpu_custom_call" | custom-call | tf_op jit(solution)/shard_map/pallas_call | solution.py:326
  98.6 0.0 copy-start
  98.6 1.5 %copy.10 = f32[128,128]{1,0:T(8,128)} copy(f32[128,128]{1,0:T(8,128)} %get-tuple-element.12) | data formatting | bytes 131072
  100.0 0.0 copy-done
  100.0 0.0 copy-start.1
  100.0 0.6 copy.11
  100.6 0.0 copy-done.1
  100.6 0.5 copy.12
Async XLA Ops:
  98.6 1.5 %copy-start = (f32[1,1024]{1,0:T(1,128)S(1)}, f32[1,1024]{1,0:T(1,128)}, u32[]{:S(2)}) copy-start(f32[1,1024]{1,0:T(1,128)} %get-tuple-element.7) | copy-start | bytes 12292
  100.0 0.6 copy-start.1

commit v2 on v1

--- a/solution.py
+++ b/solution.py
@@ -17,9 +17,9 @@
 N = 32768
 LOG_N = math.log(N)
 PAD = 144
-TC = 512
-RC = 256
-CC = 512
+TC = NC
+RC = NR
+CC = NC
 
 NT_DIMS = (((1,), (1,)), ((), ()))
 TN_DIMS = (((0,), (0,)), ((), ()))
@@ -88,7 +88,7 @@
     lax.fori_loop(1, COLS, greet_z, 0)
     src[me_z] = source_ref[...]
     tbuf[me_r, 0:D] = target_ref[...]
-    tbuf[me_r, D:PAD] = jnp.broadcast_to(potential_ref[...], (PAD - D, D)).astype(BF16)
+    tbuf[me_r, D:PAD] = jnp.broadcast_to(potential_ref[...].astype(F32).reshape(1, D), (PAD - D, D)).astype(BF16)
     paug[:, D:] = jnp.ones((NR, D), BF16)
     pl.semaphore_wait(barrier, ROWS + COLS - 2)
 
@@ -318,6 +318,12 @@
     stage_col[1] = total
     scatter_cols(1, col_in2, 8)
     col_out_ref[...] = own_col[...] + (LOG_N - jnp.log(jnp.sum(col_in2[...], axis=0)))
+
+
+def hand_over(moment_ref, row_ref, col_ref, moment_out, row_out, col_out):
+    moment_out[...] = moment_ref[...]
+    row_out[...] = row_ref[...].reshape(NR)
+    col_out[...] = col_ref[...].reshape(D)
 
 
 def per_device(source, target, target_potential, prev_moment):
@@ -363,8 +369,17 @@
         compiler_params=pltpu.CompilerParams(
             collective_id=0, has_side_effects=True, vmem_limit_bytes=58 << 20
         ),
-    )(source, target, target_potential.astype(F32).reshape(1, D), prev_moment)
-    return moment, row.reshape(NR), col.reshape(D)
+    )(source, target, target_potential, prev_moment)
+    return pl.pallas_call(
+        hand_over,
+        out_shape=(
+            jax.ShapeDtypeStruct((D, D), F32),
+            jax.ShapeDtypeStruct((NR,), F32),
+            jax.ShapeDtypeStruct((D,), F32),
+        ),
+        in_specs=[vmem] * 3,
+        out_specs=(vmem,) * 3,
+    )(moment, row, col)
 
 
 def solution(mesh):

time: 101 us -> 92.5 us (0.916)
  Pallas kernels: 96.7 us -> 91.7 us
  local copies, waits for them, and re-layouts: 2.59 us -> 0 us
  other arithmetic: 1.17 us -> 0 us
    pallas_call x1, Pallas kernels: 96.7 us -> 90.2 us  [per_device(): pl.pallas_call(kernel, out_shape=(jax.ShapeDtypeStruct((D, D), F32), jax....]
    unnamed x7 -> x0, local copies, waits for them, and re-layouts: 2.59 us -> none
    pallas_call x0 -> x1, Pallas kernels: none -> 1.48 us  [per_device(): pl.pallas_call(hand_over, out_shape=(jax.ShapeDtypeStruct((D, D), F32), j...]
    reshape x1 -> x0, other arithmetic: 1.17 us -> none  [per_device(): target_potential.astype(F32).reshape(1, D)]
where the time goes in v2:
time: 92.5 us; the launch traced here: 92.3 us
  Pallas kernels  91.7 us (99%)
    pallas_call x1, Pallas kernels, per_device(): pl.pallas_call(kernel, out_shape=(jax.ShapeDtypeStruct((D, D), F32), jax....  90.2 us

profile of v2, /device:TPU:1, one launch (start us, length us, event | category | flops | bytes accessed | tf_op | source)
XLA Modules:
  0.0 92.3 jit_solution(15033822660516175227)
XLA Ops:
  0.6 90.2 %shard_map.67 = (f32[128,128]{1,0:T(8,128)}, f32[1,1024]{1,0:T(1,128)}, f32[1,128]{1,0:T(1,128)}) custom-call(bf16[128,128]{1,0:T(8,128)(2,1)} %source_ref.1, bf16[128,128]{1,0:T(8,128)(2,1)} %target_ref.1, bf16[128]{0:T(256)(128)(2,1)} %potential_ref.1, f32[128,128]{1,0:T(8,128)} %prev_ref.1), custom_call_target="tpu_custom_call" | custom-call | tf_op jit(solution)/shard_map/pallas_call | solution.py:332
  90.8 1.5 %shard_map.68 = (f32[128,128]{1,0:T(8,128)}, f32[1024]{0:T(1024)}, f32[128]{0:T(128)}) custom-call(f32[128,128]{1,0:T(8,128)} %get-tuple-element.6.moment_ref, f32[1,1024]{1,0:T(1,128)} %get-tuple-element.7.row_ref, f32[1,128]{1,0:T(1,128)} %get-tuple-element.8.col_ref), custom_call_target="tpu_custom_call" | custom-call | tf_op jit(solution)/shard_map/pallas_call | solution.py:373

commit v3 on v2

--- a/solution.py
+++ b/solution.py
@@ -84,8 +84,8 @@
         pl.semaphore_signal(barrier, inc=1, device_id=(me_r, z_peer(k)), device_id_type=MESH)
         return _
 
-    lax.fori_loop(1, ROWS, greet_row, 0)
-    lax.fori_loop(1, COLS, greet_z, 0)
+    lax.fori_loop(1, ROWS, greet_row, 0, unroll=True)
+    lax.fori_loop(1, COLS, greet_z, 0, unroll=True)
     src[me_z] = source_ref[...]
     tbuf[me_r, 0:D] = target_ref[...]
     tbuf[me_r, D:PAD] = jnp.broadcast_to(potential_ref[...].astype(F32).reshape(1, D), (PAD - D, D)).astype(BF16)
@@ -101,8 +101,8 @@
         return _
 
     remote(tbuf.at[me_r], tbuf.at[me_r], f_send, t_recv.at[me_r], sibling, me_z).start()
-    lax.fori_loop(1, COLS, send_source, 0)
-    lax.fori_loop(1, ROWS // 2, send_target, 0)
+    lax.fori_loop(1, COLS, send_source, 0, unroll=True)
+    lax.fori_loop(1, ROWS // 2, send_target, 0, unroll=True)
 
     def forward(k, _):
         slot = plane_peer(k)
@@ -168,7 +168,7 @@
             remote(stage, inbox.at[me_z], send_sem.at[channel], recv_sem.at[channel], me_r, z_peer(k)).start()
             return _
 
-        lax.fori_loop(1, COLS, one, 0)
+        lax.fori_loop(1, COLS, one, 0, unroll=True)
         inbox[me_z] = stage[...]
 
     def wait_z(inbox, channel):
@@ -203,7 +203,7 @@
         remote(mom_stage.at[peer], mom_in.at[me_r], send_sem.at[1], recv_sem.at[1], peer, me_z).start()
         return _
 
-    lax.fori_loop(1, ROWS, send_moment, 0)
+    lax.fori_loop(1, ROWS, send_moment, 0, unroll=True)
     mom_in[me_r] = mom_stage[me_r]
     settle(mom_in.at[pl.ds(0, ROWS - 1)], recv_sem.at[1])
     settle(mom_in.at[pl.ds(0, ROWS - 1)], send_sem.at[1])
@@ -216,7 +216,7 @@
         remote(own_mom.at[1], mom_all.at[me_r], send_sem.at[3], recv_sem.at[3], row_peer(k), me_z).start()
         return _
 
-    lax.fori_loop(1, ROWS, share_moment, 0)
+    lax.fori_loop(1, ROWS, share_moment, 0, unroll=True)
     mom_all[me_r] = own_mom[1]
     settle(mom_all.at[pl.ds(0, ROWS - 1)], recv_sem.at[3])
     settle(mom_all.at[pl.ds(0, ROWS - 1)], send_sem.at[3])
@@ -271,7 +271,7 @@
             ).start()
             return _
 
-        lax.fori_loop(1, ROWS, one, 0)
+        lax.fori_loop(1, ROWS, one, 0, unroll=True)
         inbox[me_r] = stage_col[index, :, lanes(me_r)]
         settle(inbox.at[pl.ds(0, ROWS - 1)], recv_sem.at[channel])
         settle(inbox.at[pl.ds(0, ROWS - 1)], send_sem.at[channel])
@@ -283,7 +283,7 @@
         remote(own_col, col_all.at[:, lanes(me_r)], send_sem.at[6], recv_sem.at[6], row_peer(k), me_z).start()
         return _
 
-    lax.fori_loop(1, ROWS, share_col, 0)
+    lax.fori_loop(1, ROWS, share_col, 0, unroll=True)
     col_all[:, lanes(me_r)] = own_col[...]
     settle(col_all.at[:, pl.ds(0, NC - D)], recv_sem.at[6])
     settle(col_all.at[:, pl.ds(0, NC - D)], send_sem.at[6])

time: 92.5 us -> 88.1 us (0.952)
  Pallas kernels: 91.7 us -> 87.3 us
    pallas_call x1, Pallas kernels: 90.2 us -> 85.8 us  [per_device(): pl.pallas_call(kernel, out_shape=(jax.ShapeDtypeStruct((D, D), F32), jax....]
where the time goes in v3:
time: 88.1 us; the launch traced here: 88 us
  Pallas kernels  87.3 us (99%)
    pallas_call x1, Pallas kernels, per_device(): pl.pallas_call(kernel, out_shape=(jax.ShapeDtypeStruct((D, D), F32), jax....  85.8 us

profile of v3, /device:TPU:1, one launch (start us, length us, event | category | flops | bytes accessed | tf_op | source)
XLA Modules:
  0.0 88.0 jit_solution(713796320619162847)
XLA Ops:
  0.6 85.8 %shard_map.67 = (f32[128,128]{1,0:T(8,128)}, f32[1,1024]{1,0:T(1,128)}, f32[1,128]{1,0:T(1,128)}) custom-call(bf16[128,128]{1,0:T(8,128)(2,1)} %source_ref.1, bf16[128,128]{1,0:T(8,128)(2,1)} %target_ref.1, bf16[128]{0:T(256)(128)(2,1)} %potential_ref.1, f32[128,128]{1,0:T(8,128)} %prev_ref.1), custom_call_target="tpu_custom_call" | custom-call | tf_op jit(solution)/shard_map/pallas_call | solution.py:332
  86.5 1.5 %shard_map.68 = (f32[128,128]{1,0:T(8,128)}, f32[1024]{0:T(1024)}, f32[128]{0:T(128)}) custom-call(f32[128,128]{1,0:T(8,128)} %get-tuple-element.6.moment_ref, f32[1,1024]{1,0:T(1,128)} %get-tuple-element.7.row_ref, f32[1,128]{1,0:T(1,128)} %get-tuple-element.8.col_ref), custom_call_target="tpu_custom_call" | custom-call | tf_op jit(solution)/shard_map/pallas_call | solution.py:373

commit v4 on v3

--- a/solution.py
+++ b/solution.py
@@ -16,6 +16,10 @@
 NC = 4096
 N = 32768
 LOG_N = math.log(N)
+PLANE = sorted(((x, y) for x in range(4) for y in range(4)), key=lambda o: -(min(o[0], 4 - o[0]) + min(o[1], 4 - o[1])))
+ROW_PEERS = [(x, y, c) for x, y in PLANE for c in (0, 1) if (x, y, c) != (0, 0, 0)]
+PLANE_PEERS = [(x, y, 0) for x, y in PLANE if (x, y) != (0, 0)]
+Z_PEERS = [4, 3, 5, 2, 6, 1, 7]
 PAD = 144
 TC = NC
 RC = NR
@@ -30,6 +34,11 @@
     rest = value - high.astype(F32)
     middle = rest.astype(BF16)
     return high, middle, (rest - middle.astype(F32)).astype(BF16)
+
+
+def for_each(start, partners):
+    for partner in partners:
+        start(partner, 0)
 
 
 def dot_nt(a, b):
@@ -56,8 +65,12 @@
     chip = lax.div(me_r, 2)
     sibling = chip * 2 + (1 - core)
 
-    def row_peer(k):
-        return lax.rem(me_r + k, ROWS)
+    chip_x, chip_y = lax.div(chip, 4), lax.rem(chip, 4)
+
+    def row_peer(offset):
+        dx, dy, dc = offset
+        at = lax.rem(chip_x + dx, 4) * 4 + lax.rem(chip_y + dy, 4)
+        return at * 2 + (1 - core if dc else core)
 
     def z_peer(k):
         return lax.rem(me_z + k, COLS)
@@ -84,8 +97,8 @@
         pl.semaphore_signal(barrier, inc=1, device_id=(me_r, z_peer(k)), device_id_type=MESH)
         return _
 
-    lax.fori_loop(1, ROWS, greet_row, 0, unroll=True)
-    lax.fori_loop(1, COLS, greet_z, 0, unroll=True)
+    for_each(greet_row, ROW_PEERS)
+    for_each(greet_z, Z_PEERS)
     src[me_z] = source_ref[...]
     tbuf[me_r, 0:D] = target_ref[...]
     tbuf[me_r, D:PAD] = jnp.broadcast_to(potential_ref[...].astype(F32).reshape(1, D), (PAD - D, D)).astype(BF16)
@@ -97,17 +110,28 @@
         return _
 
     def send_target(k, _):
-        remote(tbuf.at[me_r], tbuf.at[me_r], t_send, t_recv.at[me_r], plane_peer(k), me_z).start()
+        remote(tbuf.at[me_r], tbuf.at[me_r], t_send, t_recv.at[me_r], row_peer(k), me_z).start()
         return _
 
     remote(tbuf.at[me_r], tbuf.at[me_r], f_send, t_recv.at[me_r], sibling, me_z).start()
-    lax.fori_loop(1, COLS, send_source, 0, unroll=True)
-    lax.fori_loop(1, ROWS // 2, send_target, 0, unroll=True)
+    for_each(send_source, Z_PEERS)
+    for_each(send_target, PLANE_PEERS)
+
+    eye = lax.broadcasted_iota(jnp.int32, (D, D), 0) == lax.broadcasted_iota(jnp.int32, (D, D), 1)
+
+    def place(slot):
+        block = tbuf[slot]
+        at = pl.ds(pl.multiple_of(slot * D, D), D)
+        taug[at, 0:D] = block[0:D]
+        taug[at, D:] = jnp.where(eye, block[D : D + 1].astype(F32), 0.0).astype(BF16)
+
+    place(me_r)
 
     def forward(k, _):
         slot = plane_peer(k)
         settle(tbuf.at[slot], t_recv.at[slot])
         remote(tbuf.at[slot], tbuf.at[slot], f_send, t_recv.at[slot], sibling, me_z).start()
+        place(slot)
         return _
 
     lax.fori_loop(1, ROWS // 2, forward, 0)
@@ -121,30 +145,20 @@
         paug[:, 0:D] = (4.0 * total).astype(BF16)
 
     def project_prev(rows):
-        high, middle, low = split3(prev_ref[...])
-        return dot_nn(rows, high) + (dot_nn(rows, middle) + dot_nn(rows, low))
+        wide = dot_nn(rows, jnp.concatenate(split3(prev_ref[...]), axis=1))
+        return wide[:, 0:D] + (wide[:, D : 2 * D] + wide[:, 2 * D :])
 
     project(project_prev)
 
     def arrive(k, _):
         slot = lax.rem(chip + k, ROWS // 2) * 2 + (1 - core)
         settle(tbuf.at[slot], t_recv.at[slot])
+        place(slot)
         return _
 
     lax.fori_loop(0, ROWS // 2, arrive, 0)
     settle(tbuf.at[pl.ds(0, ROWS // 2 - 1)], t_send)
     settle(tbuf.at[pl.ds(0, ROWS // 2)], f_send)
-
-    eye = lax.broadcasted_iota(jnp.int32, (D, D), 0) == lax.broadcasted_iota(jnp.int32, (D, D), 1)
-
-    def place(k, _):
-        block = tbuf[k]
-        at = pl.ds(pl.multiple_of(k * D, D), D)
-        taug[at, 0:D] = block[0:D]
-        taug[at, D:] = jnp.where(eye, block[D : D + 1].astype(F32), 0.0).astype(BF16)
-        return _
-
-    lax.fori_loop(0, ROWS, place, 0)
 
     def row_pass(keep):
         def step(c, carry):
@@ -168,7 +182,7 @@
             remote(stage, inbox.at[me_z], send_sem.at[channel], recv_sem.at[channel], me_r, z_peer(k)).start()
             return _
 
-        lax.fori_loop(1, COLS, one, 0, unroll=True)
+        for_each(one, Z_PEERS)
         inbox[me_z] = stage[...]
 
     def wait_z(inbox, channel):
@@ -193,8 +207,8 @@
     wait_z(row_in1, 0)
     carried = carried * (jnp.exp(top - total_lse(row_in1)) / N)
     rows = src[...].reshape(NR, D)
-    high, middle, low = split3(carried)
-    part_moment = dot_nn(high, rows) + (dot_nn(middle, rows) + dot_nn(low, rows))
+    tall = dot_nn(jnp.concatenate(split3(carried), axis=0), rows)
+    part_moment = tall[0:D] + (tall[D : 2 * D] + tall[2 * D :])
     for k in range(ROWS):
         mom_stage[k] = part_moment[4 * k : 4 * k + 4]
 
@@ -203,7 +217,7 @@
         remote(mom_stage.at[peer], mom_in.at[me_r], send_sem.at[1], recv_sem.at[1], peer, me_z).start()
         return _
 
-    lax.fori_loop(1, ROWS, send_moment, 0, unroll=True)
+    for_each(send_moment, ROW_PEERS)
     mom_in[me_r] = mom_stage[me_r]
     settle(mom_in.at[pl.ds(0, ROWS - 1)], recv_sem.at[1])
     settle(mom_in.at[pl.ds(0, ROWS - 1)], send_sem.at[1])
@@ -216,7 +230,7 @@
         remote(own_mom.at[1], mom_all.at[me_r], send_sem.at[3], recv_sem.at[3], row_peer(k), me_z).start()
         return _
 
-    lax.fori_loop(1, ROWS, share_moment, 0, unroll=True)
+    for_each(share_moment, ROW_PEERS)
     mom_all[me_r] = own_mom[1]
     settle(mom_all.at[pl.ds(0, ROWS - 1)], recv_sem.at[3])
     settle(mom_all.at[pl.ds(0, ROWS - 1)], send_sem.at[3])
@@ -225,8 +239,8 @@
     moment_t = moment_ref[...]
 
     def project_new(block):
-        first, second, third = split3(moment_t)
-        return dot_nt(block, first) + (dot_nt(block, second) + dot_nt(block, third))
+        wide = dot_nt(block, jnp.concatenate(split3(moment_t), axis=0))
+        return wide[:, 0:D] + (wide[:, D : 2 * D] + wide[:, 2 * D :])
 
     project(project_new)
     moment_ref[...] = moment_t.T
@@ -271,7 +285,7 @@
             ).start()
             return _
 
-        lax.fori_loop(1, ROWS, one, 0, unroll=True)
+        for_each(one, ROW_PEERS)
         inbox[me_r] = stage_col[index, :, lanes(me_r)]
         settle(inbox.at[pl.ds(0, ROWS - 1)], recv_sem.at[channel])
         settle(inbox.at[pl.ds(0, ROWS - 1)], send_sem.at[channel])
@@ -283,7 +297,7 @@
         remote(own_col, col_all.at[:, lanes(me_r)], send_sem.at[6], recv_sem.at[6], row_peer(k), me_z).start()
         return _
 
-    lax.fori_loop(1, ROWS, share_col, 0, unroll=True)
+    for_each(share_col, ROW_PEERS)
     col_all[:, lanes(me_r)] = own_col[...]
     settle(col_all.at[:, pl.ds(0, NC - D)], recv_sem.at[6])
     settle(col_all.at[:, pl.ds(0, NC - D)], send_sem.at[6])

time: 88.1 us -> 84.8 us (0.963)
  Pallas kernels: 87.3 us -> 84 us
    pallas_call x1, Pallas kernels: 85.8 us -> 82.5 us  [per_device(): pl.pallas_call(kernel, out_shape=(jax.ShapeDtypeStruct((D, D), F32), jax....]
where the time goes in v4:
time: 84.8 us; the launch traced here: 84.7 us
  Pallas kernels  84 us (99%)
    pallas_call x1, Pallas kernels, per_device(): pl.pallas_call(kernel, out_shape=(jax.ShapeDtypeStruct((D, D), F32), jax....  82.5 us

profile of v4, /device:TPU:1, one launch (start us, length us, event | category | flops | bytes accessed | tf_op | source)
XLA Modules:
  0.0 84.7 jit_solution(3746665504323770647)
XLA Ops:
  0.6 82.5 %shard_map.67 = (f32[128,128]{1,0:T(8,128)}, f32[1,1024]{1,0:T(1,128)}, f32[1,128]{1,0:T(1,128)}) custom-call(bf16[128,128]{1,0:T(8,128)(2,1)} %source_ref.1, bf16[128,128]{1,0:T(8,128)(2,1)} %target_ref.1, bf16[128]{0:T(256)(128)(2,1)} %potential_ref.1, f32[128,128]{1,0:T(8,128)} %prev_ref.1), custom_call_target="tpu_custom_call" | custom-call | tf_op jit(solution)/shard_map/pallas_call | solution.py:346
  83.2 1.5 %shard_map.68 = (f32[128,128]{1,0:T(8,128)}, f32[1024]{0:T(1024)}, f32[128]{0:T(128)}) custom-call(f32[128,128]{1,0:T(8,128)} %get-tuple-element.6.moment_ref, f32[1,1024]{1,0:T(1,128)} %get-tuple-element.7.row_ref, f32[1,128]{1,0:T(1,128)} %get-tuple-element.8.col_ref), custom_call_target="tpu_custom_call" | custom-call | tf_op jit(solution)/shard_map/pallas_call | solution.py:387

commit v5 on v4

--- a/solution.py
+++ b/solution.py
@@ -75,9 +75,6 @@
     def z_peer(k):
         return lax.rem(me_z + k, COLS)
 
-    def plane_peer(k):
-        return lax.rem(chip + k, ROWS // 2) * 2 + core
-
     def remote(source, dest, send, recv, row, col):
         return pltpu.make_async_remote_copy(
             src_ref=source, dst_ref=dest, send_sem=send, recv_sem=recv,
@@ -128,13 +125,13 @@
     place(me_r)
 
     def forward(k, _):
-        slot = plane_peer(k)
+        slot = row_peer(k)
         settle(tbuf.at[slot], t_recv.at[slot])
         remote(tbuf.at[slot], tbuf.at[slot], f_send, t_recv.at[slot], sibling, me_z).start()
         place(slot)
         return _
 
-    lax.fori_loop(1, ROWS // 2, forward, 0)
+    for_each(forward, PLANE_PEERS[::-1])
 
     settle(src.at[pl.ds(0, COLS - 1)], src_recv)
     settle(src.at[pl.ds(0, COLS - 1)], src_send)
@@ -151,12 +148,12 @@
     project(project_prev)
 
     def arrive(k, _):
-        slot = lax.rem(chip + k, ROWS // 2) * 2 + (1 - core)
+        slot = row_peer(k)
         settle(tbuf.at[slot], t_recv.at[slot])
         place(slot)
         return _
 
-    lax.fori_loop(0, ROWS // 2, arrive, 0)
+    for_each(arrive, [(x, y, 1) for x, y in PLANE[::-1]])
     settle(tbuf.at[pl.ds(0, ROWS // 2 - 1)], t_send)
     settle(tbuf.at[pl.ds(0, ROWS // 2)], f_send)
 
@@ -269,9 +266,7 @@
         return _
 
     lax.fori_loop(0, (NR // RC) * (NC // CC), col_step, 0)
-    tops = col_top[...]
-    best = jnp.max(tops, axis=0)
-    stage_col[0] = best + jnp.log(jnp.sum(col_mass[...] * jnp.exp(tops - best[None]), axis=0))
+    stage_col[0] = col_top[0] + jnp.log(col_mass[0])
 
     def lanes(k):
         return pl.ds(pl.multiple_of(k * D, D), D)

time: 84.8 us -> 84.6 us (level)
  no operation moved by 1% of the time
where the time goes in v5:
time: 84.6 us; the launch traced here: 84.4 us
  Pallas kernels  83.8 us (99%)
    pallas_call x1, Pallas kernels, per_device(): pl.pallas_call(kernel, out_shape=(jax.ShapeDtypeStruct((D, D), F32), jax....  82.3 us

profile of v5, /device:TPU:1, one launch (start us, length us, event | category | flops | bytes accessed | tf_op | source)
XLA Modules:
  0.0 84.4 jit_solution(4058155257944002458)
XLA Ops:
  0.6 82.3 %shard_map.67 = (f32[128,128]{1,0:T(8,128)}, f32[1,1024]{1,0:T(1,128)}, f32[1,128]{1,0:T(1,128)}) custom-call(bf16[128,128]{1,0:T(8,128)(2,1)} %source_ref.1, bf16[128,128]{1,0:T(8,128)(2,1)} %target_ref.1, bf16[128]{0:T(256)(128)(2,1)} %potential_ref.1, f32[128,128]{1,0:T(8,128)} %prev_ref.1), custom_call_target="tpu_custom_call" | custom-call | tf_op jit(solution)/shard_map/pallas_call | solution.py:341
  82.9 1.5 %shard_map.68 = (f32[128,128]{1,0:T(8,128)}, f32[1024]{0:T(1024)}, f32[128]{0:T(128)}) custom-call(f32[128,128]{1,0:T(8,128)} %get-tuple-element.6.moment_ref, f32[1,1024]{1,0:T(1,128)} %get-tuple-element.7.row_ref, f32[1,128]{1,0:T(1,128)} %get-tuple-element.8.col_ref), custom_call_target="tpu_custom_call" | custom-call | tf_op jit(solution)/shard_map/pallas_call | solution.py:382
